TPU v7x, 32 devices: a whole 2x2x4 slice. The times are simulated.
32 devices in a mesh: section: 8 (over y, x, core), dp: 4 (over z).
Axes of the slice: x: 2, y: 2, z: 4, core: 2. Of those that a mesh axis runs over, the one named last changes fastest.
Arguments:
- images: bfloat16 [12, 256, 512], P(None, 'dp'), may hold values from -6 to 6
- cotangent: bfloat16 [12, 256, 512], P(None, 'dp'), may hold values from -6 to 6
- w_in: bfloat16 [8, 4, 512, 512], P('section', None, 'dp'), may hold values from -0.25 to 0.25
- w_out: bfloat16 [8, 4, 512, 512], P('section', None, 'dp'), may hold values from -0.0625 to 0.0625
Outputs:
- new_in: float32 [8, 4, 512, 512], P('section', None, 'dp')
- new_out: float32 [8, 4, 512, 512], P('section', None, 'dp')
All inputs are finite; a program needn't handle non-finite values.
Results may differ from a plain program's by a relative error of at most 0.03.
Values may be sent and summed in bfloat16 or wider, within the bound.
A program may use at most 128 MiB of HBM per device.

v0:
```python
import math
import jax
import jax.numpy as jnp
from jax import lax
from jax.sharding import PartitionSpec as P


def shifted(value, axis, steps):
    count = lax.axis_size(axis)
    initial, last = (max(0, -steps), min(count, count - steps))
    return lax.ppermute(value, axis, [(source, source + steps) for source in range(initial, last)])


def per_device(images, cotangent, w_in, w_out):
    sections = lax.axis_size("section")
    place = lax.axis_index("section")
    groups = lax.axis_size("dp")
    full_in, full_out = (
        lax.all_gather(w_in, "dp", axis=2, tiled=True),
        lax.all_gather(w_out, "dp", axis=2, tiled=True),
    )
    first = full_in[0]
    second = full_out[0]
    micro, rows, width = images.shape
    layers = first.shape[0]
    ticks = micro + sections - 1
    zero_rows = jnp.zeros((rows, width), jnp.bfloat16)
    zero_stack = jnp.zeros((layers, rows, width), jnp.bfloat16)
    contract = (((1,), (1,)), ((), ()))

    def forward_section(value):
        inputs = []
        for layer in range(layers):
            inputs.append(value)
            pre = jnp.dot(value, first[layer], preferred_element_type=jnp.float32)
            hidden = (pre * jax.nn.sigmoid(pre)).astype(jnp.bfloat16)
            value = (
                value.astype(jnp.float32)
                + jnp.dot(hidden, second[layer], preferred_element_type=jnp.float32)
            ).astype(jnp.bfloat16)
        return (value, jnp.stack(inputs))

    def backward_section(inputs, grad):
        hiddens, dpres, grads = ([], [], [])
        for layer in reversed(range(layers)):
            value = inputs[layer]
            pre = jnp.dot(value, first[layer], preferred_element_type=jnp.float32)
            sig = jax.nn.sigmoid(pre)
            hiddens.append((pre * sig).astype(jnp.bfloat16))
            grads.append(grad)
            dhidden = lax.dot_general(
                grad, second[layer], contract, preferred_element_type=jnp.float32
            )
            dpre = (dhidden * (sig * (1.0 + pre * (1.0 - sig)))).astype(jnp.bfloat16)
            dpres.append(dpre)
            grad = (
                grad.astype(jnp.float32)
                + lax.dot_general(dpre, first[layer], contract, preferred_element_type=jnp.float32)
            ).astype(jnp.bfloat16)
        return (grad, jnp.stack(hiddens[::-1]), jnp.stack(dpres[::-1]), jnp.stack(grads[::-1]))

    def put(store, index, valid, fresh, axis_pos):
        old = lax.dynamic_index_in_dim(store, index, axis_pos, keepdims=False)
        return lax.dynamic_update_index_in_dim(store, jnp.where(valid, fresh, old), index, axis_pos)

    kept0 = jnp.zeros((layers, micro, rows, width), jnp.bfloat16)

    def forward_tick(carry, tick):
        incoming, kept = carry
        slot = tick - place
        valid = (slot >= 0) & (slot < micro)
        index = jnp.clip(slot, 0, micro - 1)
        fresh = lax.dynamic_index_in_dim(images, index, 0, keepdims=False)
        source = jnp.where(place == 0, fresh, incoming)
        output, inputs = lax.cond(
            valid, lambda: forward_section(source), lambda: (zero_rows, zero_stack)
        )
        kept = put(kept, index, valid, inputs, 1)
        passed = shifted(output, "section", 1)
        return ((passed, kept), None)

    (unused_in, kept), unused = lax.scan(
        forward_tick, (zero_rows, kept0), jnp.arange(ticks, dtype=jnp.int32)
    )

    def relay_step(tick, incoming):
        slot = tick - (sections - 1 - place)
        valid = (slot >= 0) & (slot < micro)
        index = jnp.clip(slot, 0, micro - 1)
        fresh = lax.dynamic_index_in_dim(cotangent, index, 0, keepdims=False)
        upstream = jnp.where(place == sections - 1, fresh, incoming)
        inputs = lax.dynamic_index_in_dim(kept, index, 1, keepdims=False)

        def run():
            back, hiddens, dpres, grads = backward_section(inputs, upstream)
            return (back, hiddens, dpres, grads)

        back, hiddens, dpres, grads = lax.cond(
            valid, run, lambda: (zero_rows, zero_stack, zero_stack, zero_stack)
        )
        passed = shifted(back, "section", -1)
        return (passed, valid, index, inputs, hiddens, dpres, grads)

    blank = jnp.zeros((layers, micro, rows, width), jnp.bfloat16)

    def backward_tick(carry, tick):
        incoming, hidden_all, dpre_all, grad_all = carry
        passed, valid, index, inputs, hiddens, dpres, grads = relay_step(tick, incoming)
        hidden_all = put(hidden_all, index, valid, hiddens, 1)
        dpre_all = put(dpre_all, index, valid, dpres, 1)
        grad_all = put(grad_all, index, valid, grads, 1)
        return ((passed, hidden_all, dpre_all, grad_all), None)

    (unused_back, hidden_all, dpre_all, grad_all), unused = lax.scan(
        backward_tick, (zero_rows, blank, blank, blank), jnp.arange(ticks, dtype=jnp.int32)
    )
    flat_inputs = kept.reshape(layers, micro * rows, width)
    flat_hidden = hidden_all.reshape(layers, micro * rows, width)
    flat_dpre = dpre_all.reshape(layers, micro * rows, width)
    flat_grad = grad_all.reshape(layers, micro * rows, width)
    grad_in = None
    grad_out = None
    grad_in = jnp.einsum("lrc,lrd->lcd", flat_inputs, flat_dpre, preferred_element_type=jnp.float32)
    grad_out = jnp.einsum(
        "lrc,lrd->lcd", flat_hidden, flat_grad, preferred_element_type=jnp.float32
    )
    share_in, share_out = (
        lax.psum_scatter(grad_in, "dp", scatter_dimension=1, tiled=True),
        lax.psum_scatter(grad_out, "dp", scatter_dimension=1, tiled=True),
    )
    rate = 0.1 / math.sqrt(micro * rows * groups)
    new_in = w_in.astype(jnp.float32) - rate * share_in[None]
    new_out = w_out.astype(jnp.float32) - rate * share_out[None]
    return (new_in, new_out)


def solution(mesh):
    in_specs = (
        P(None, "dp", None),
        P(None, "dp", None),
        P("section", None, "dp", None),
        P("section", None, "dp", None),
    )
    out_specs = (P("section", None, "dp", None), P("section", None, "dp", None))
    return jax.shard_map(
        per_device, mesh=mesh, in_specs=in_specs, out_specs=out_specs, check_vma=False
    )
```

profile of v0, /device:TPU:0, one launch (start us, length us, event | category | flops | bytes accessed | tf_op | source)
XLA Modules:
  0.0 829.8 jit_solution(466928142596177172)
XLA Ops:
  8.7 49.5 %all-gather.3.cloned.1.call-done = bf16[1,4,512,512]{3,2,1,0:T(8,128)(2,1)} async-done(((bf16[1,4,128,512]{3,2,1,0:T(8,128)(2,1)}), bf16[1,4,512,512]{3,2,1,0:T(8,128)(2,1)}) %all-gather.3.cloned.1.call-update) | async-done | bytes 2097168 | tf_op jit(solution)/shard_map/all_gather | solution.py:19
  58.2 46.3 %all-gather.5.cloned.1.call-done = bf16[1,4,512,512]{3,2,1,0:T(8,128)(2,1)} async-done(((bf16[1,4,128,512]{3,2,1,0:T(8,128)(2,1)}), bf16[1,4,512,512]{3,2,1,0:T(8,128)(2,1)}) %all-gather.5.cloned.1.call-update) | async-done | bytes 2097168 | tf_op jit(solution)/shard_map/all_gather | solution.py:20
  106.5 235.0 %while.31 = (s32[]{:T(128)}, bf16[64,512]{1,0:T(8,128)(2,1)S(1)}, bf16[4,12,64,512]{3,2,1,0:T(8,128)(2,1)}, s32[19]{0:T(128)S(1)}, s32[]{:T(128)}, /*index=5*/pr...) while((s32[]{:T(128)}, bf16[64,512]{1,0:T(8,128)(2,1)S(1)}, ...), condition=%wide.region_3.4_spmd, body=%wide.region_0.3_spmd.sunk | while | flops 270106624 | bytes 7408441 | solution.py:82
  155.1 6.7 conditional.4
  263.4 10.5 %collective-permute-start = (bf16[64,512]{1,0:T(8,128)(2,1)S(1)}, bf16[64,512]{1,0:T(8,128)(2,1)S(1)}, u32[]{:S(2)}, u32[]{:S(2)}) collective-permute-start(bf16[64,512]{1,0:T(8,128)(2,1)S(1)} %get-tuple-element.520), channel_id=1, source_target_pairs={{0,4},{4,8},{8,12},{12,16},{16,20},{20,24},{24,28},{1,5},{5,9},{9,... | collective-permute-start | bytes 196616 | tf_op jit(solution)/shard_map/while/body/eval_jaxpr/ppermute | solution.py:11
  283.9 11.3 %collective-permute-start = (bf16[64,512]{1,0:T(8,128)(2,1)S(1)}, bf16[64,512]{1,0:T(8,128)(2,1)S(1)}, u32[]{:S(2)}, u32[]{:S(2)}) collective-permute-start(bf16[64,512]{1,0:T(8,128)(2,1)S(1)} %get-tuple-element.520), channel_id=1, source_target_pairs={{0,4},{4,8},{8,12},{12,16},{16,20},{20,24},{24,28},{1,5},{5,9},{9,... | collective-permute-start | bytes 196616 | tf_op jit(solution)/shard_map/while/body/eval_jaxpr/ppermute | solution.py:11
  306.2 11.3 %collective-permute-start = (bf16[64,512]{1,0:T(8,128)(2,1)S(1)}, bf16[64,512]{1,0:T(8,128)(2,1)S(1)}, u32[]{:S(2)}, u32[]{:S(2)}) collective-permute-start(bf16[64,512]{1,0:T(8,128)(2,1)S(1)} %get-tuple-element.520), channel_id=1, source_target_pairs={{0,4},{4,8},{8,12},{12,16},{16,20},{20,24},{24,28},{1,5},{5,9},{9,... | collective-permute-start | bytes 196616 | tf_op jit(solution)/shard_map/while/body/eval_jaxpr/ppermute | solution.py:11
  328.5 11.3 %collective-permute-start = (bf16[64,512]{1,0:T(8,128)(2,1)S(1)}, bf16[64,512]{1,0:T(8,128)(2,1)S(1)}, u32[]{:S(2)}, u32[]{:S(2)}) collective-permute-start(bf16[64,512]{1,0:T(8,128)(2,1)S(1)} %get-tuple-element.520), channel_id=1, source_target_pairs={{0,4},{4,8},{8,12},{12,16},{16,20},{20,24},{24,28},{1,5},{5,9},{9,... | collective-permute-start | bytes 196616 | tf_op jit(solution)/shard_map/while/body/eval_jaxpr/ppermute | solution.py:11
  347.8 312.3 %while.32 = (s32[]{:T(128)}, bf16[64,512]{1,0:T(8,128)(2,1)S(1)}, bf16[4,12,64,512]{3,2,1,0:T(8,128)(2,1)}, bf16[4,12,64,512]{3,2,1,0:T(8,128)(2,1)}, bf16[4,12,...) while((s32[]{:T(128)}, bf16[64,512]{1,0:T(8,128)(2,1)S(1)}, ...), condition=%wide.region_7.8_spmd, body=%wide.region_4.7_spmd.sunk | while | flops 406487040 | bytes 24055228 | solution.py:114
  404.1 56.2 %collective-permute-done.1 = bf16[64,512]{1,0:T(8,128)(2,1)S(1)} collective-permute-done((bf16[64,512]{1,0:T(8,128)(2,1)S(1)}, bf16[64,512]{1,0:T(8,128)(2,1)S(1)}, u32[]{:S(2)}, u32[]{:S(2)}) %collective-permute-start.1) | collective-permute-done | bytes 65568 | tf_op jit(solution)/shard_map/while/body/eval_jaxpr/ppermute | solution.py:11
  461.5 8.9 %conditional.5 = (bf16[64,512]{1,0:T(8,128)(2,1)S(1)}, bf16[4,64,512]{2,1,0:T(8,128)(2,1)S(1)}, bf16[4,64,512]{2,1,0:T(8,128)(2,1)S(1)}, bf16[4,64,512]{2,1,0:T(8,128)(2,1)S(1)}) conditional(s32[]{:T(128)} %convert_element_type.194, () %tuple.83, (pred[]{:T(512)}, bf16[12,64,512]{2,1,0:T(8,128)(2,1)}, s32[]{:T(128)}, bf16[64,512]{1,0:T(8,128)(2,1)S(1)}, ...), branch_computations={%region_5.5_spmd, %region_6.6_spmd} | conditional | flops 406093824 | bytes 19859568 | solution.py:98
  478.2 8.9 %conditional.5 = (bf16[64,512]{1,0:T(8,128)(2,1)S(1)}, bf16[4,64,512]{2,1,0:T(8,128)(2,1)S(1)}, bf16[4,64,512]{2,1,0:T(8,128)(2,1)S(1)}, bf16[4,64,512]{2,1,0:T(8,128)(2,1)S(1)}) conditional(s32[]{:T(128)} %convert_element_type.194, () %tuple.83, (pred[]{:T(512)}, bf16[12,64,512]{2,1,0:T(8,128)(2,1)}, s32[]{:T(128)}, bf16[64,512]{1,0:T(8,128)(2,1)S(1)}, ...), branch_computations={%region_5.5_spmd, %region_6.6_spmd} | conditional | flops 406093824 | bytes 19859568 | solution.py:98
  494.9 8.9 %conditional.5 = (bf16[64,512]{1,0:T(8,128)(2,1)S(1)}, bf16[4,64,512]{2,1,0:T(8,128)(2,1)S(1)}, bf16[4,64,512]{2,1,0:T(8,128)(2,1)S(1)}, bf16[4,64,512]{2,1,0:T(8,128)(2,1)S(1)}) conditional(s32[]{:T(128)} %convert_element_type.194, () %tuple.83, (pred[]{:T(512)}, bf16[12,64,512]{2,1,0:T(8,128)(2,1)}, s32[]{:T(128)}, bf16[64,512]{1,0:T(8,128)(2,1)S(1)}, ...), branch_computations={%region_5.5_spmd, %region_6.6_spmd} | conditional | flops 406093824 | bytes 19859568 | solution.py:98
  511.6 8.9 %conditional.5 = (bf16[64,512]{1,0:T(8,128)(2,1)S(1)}, bf16[4,64,512]{2,1,0:T(8,128)(2,1)S(1)}, bf16[4,64,512]{2,1,0:T(8,128)(2,1)S(1)}, bf16[4,64,512]{2,1,0:T(8,128)(2,1)S(1)}) conditional(s32[]{:T(128)} %convert_element_type.194, () %tuple.83, (pred[]{:T(512)}, bf16[12,64,512]{2,1,0:T(8,128)(2,1)}, s32[]{:T(128)}, bf16[64,512]{1,0:T(8,128)(2,1)S(1)}, ...), branch_computations={%region_5.5_spmd, %region_6.6_spmd} | conditional | flops 406093824 | bytes 19859568 | solution.py:98
  528.3 8.9 %conditional.5 = (bf16[64,512]{1,0:T(8,128)(2,1)S(1)}, bf16[4,64,512]{2,1,0:T(8,128)(2,1)S(1)}, bf16[4,64,512]{2,1,0:T(8,128)(2,1)S(1)}, bf16[4,64,512]{2,1,0:T(8,128)(2,1)S(1)}) conditional(s32[]{:T(128)} %convert_element_type.194, () %tuple.83, (pred[]{:T(512)}, bf16[12,64,512]{2,1,0:T(8,128)(2,1)}, s32[]{:T(128)}, bf16[64,512]{1,0:T(8,128)(2,1)S(1)}, ...), branch_computations={%region_5.5_spmd, %region_6.6_spmd} | conditional | flops 406093824 | bytes 19859568 | solution.py:98
  545.0 8.9 %conditional.5 = (bf16[64,512]{1,0:T(8,128)(2,1)S(1)}, bf16[4,64,512]{2,1,0:T(8,128)(2,1)S(1)}, bf16[4,64,512]{2,1,0:T(8,128)(2,1)S(1)}, bf16[4,64,512]{2,1,0:T(8,128)(2,1)S(1)}) conditional(s32[]{:T(128)} %convert_element_type.194, () %tuple.83, (pred[]{:T(512)}, bf16[12,64,512]{2,1,0:T(8,128)(2,1)}, s32[]{:T(128)}, bf16[64,512]{1,0:T(8,128)(2,1)S(1)}, ...), branch_computations={%region_5.5_spmd, %region_6.6_spmd} | conditional | flops 406093824 | bytes 19859568 | solution.py:98
  561.7 8.9 %conditional.5 = (bf16[64,512]{1,0:T(8,128)(2,1)S(1)}, bf16[4,64,512]{2,1,0:T(8,128)(2,1)S(1)}, bf16[4,64,512]{2,1,0:T(8,128)(2,1)S(1)}, bf16[4,64,512]{2,1,0:T(8,128)(2,1)S(1)}) conditional(s32[]{:T(128)} %convert_element_type.194, () %tuple.83, (pred[]{:T(512)}, bf16[12,64,512]{2,1,0:T(8,128)(2,1)}, s32[]{:T(128)}, bf16[64,512]{1,0:T(8,128)(2,1)S(1)}, ...), branch_computations={%region_5.5_spmd, %region_6.6_spmd} | conditional | flops 406093824 | bytes 19859568 | solution.py:98
  578.4 8.9 %conditional.5 = (bf16[64,512]{1,0:T(8,128)(2,1)S(1)}, bf16[4,64,512]{2,1,0:T(8,128)(2,1)S(1)}, bf16[4,64,512]{2,1,0:T(8,128)(2,1)S(1)}, bf16[4,64,512]{2,1,0:T(8,128)(2,1)S(1)}) conditional(s32[]{:T(128)} %convert_element_type.194, () %tuple.83, (pred[]{:T(512)}, bf16[12,64,512]{2,1,0:T(8,128)(2,1)}, s32[]{:T(128)}, bf16[64,512]{1,0:T(8,128)(2,1)S(1)}, ...), branch_computations={%region_5.5_spmd, %region_6.6_spmd} | conditional | flops 406093824 | bytes 19859568 | solution.py:98
  595.1 8.9 %conditional.5 = (bf16[64,512]{1,0:T(8,128)(2,1)S(1)}, bf16[4,64,512]{2,1,0:T(8,128)(2,1)S(1)}, bf16[4,64,512]{2,1,0:T(8,128)(2,1)S(1)}, bf16[4,64,512]{2,1,0:T(8,128)(2,1)S(1)}) conditional(s32[]{:T(128)} %convert_element_type.194, () %tuple.83, (pred[]{:T(512)}, bf16[12,64,512]{2,1,0:T(8,128)(2,1)}, s32[]{:T(128)}, bf16[64,512]{1,0:T(8,128)(2,1)S(1)}, ...), branch_computations={%region_5.5_spmd, %region_6.6_spmd} | conditional | flops 406093824 | bytes 19859568 | solution.py:98
  611.9 8.9 %conditional.5 = (bf16[64,512]{1,0:T(8,128)(2,1)S(1)}, bf16[4,64,512]{2,1,0:T(8,128)(2,1)S(1)}, bf16[4,64,512]{2,1,0:T(8,128)(2,1)S(1)}, bf16[4,64,512]{2,1,0:T(8,128)(2,1)S(1)}) conditional(s32[]{:T(128)} %convert_element_type.194, () %tuple.83, (pred[]{:T(512)}, bf16[12,64,512]{2,1,0:T(8,128)(2,1)}, s32[]{:T(128)}, bf16[64,512]{1,0:T(8,128)(2,1)S(1)}, ...), branch_computations={%region_5.5_spmd, %region_6.6_spmd} | conditional | flops 406093824 | bytes 19859568 | solution.py:98
  628.5 8.9 %conditional.5 = (bf16[64,512]{1,0:T(8,128)(2,1)S(1)}, bf16[4,64,512]{2,1,0:T(8,128)(2,1)S(1)}, bf16[4,64,512]{2,1,0:T(8,128)(2,1)S(1)}, bf16[4,64,512]{2,1,0:T(8,128)(2,1)S(1)}) conditional(s32[]{:T(128)} %convert_element_type.194, () %tuple.83, (pred[]{:T(512)}, bf16[12,64,512]{2,1,0:T(8,128)(2,1)}, s32[]{:T(128)}, bf16[64,512]{1,0:T(8,128)(2,1)S(1)}, ...), branch_computations={%region_5.5_spmd, %region_6.6_spmd} | conditional | flops 406093824 | bytes 19859568 | solution.py:98
  645.2 8.9 %conditional.5 = (bf16[64,512]{1,0:T(8,128)(2,1)S(1)}, bf16[4,64,512]{2,1,0:T(8,128)(2,1)S(1)}, bf16[4,64,512]{2,1,0:T(8,128)(2,1)S(1)}, bf16[4,64,512]{2,1,0:T(8,128)(2,1)S(1)}) conditional(s32[]{:T(128)} %convert_element_type.194, () %tuple.83, (pred[]{:T(512)}, bf16[12,64,512]{2,1,0:T(8,128)(2,1)}, s32[]{:T(128)}, bf16[64,512]{1,0:T(8,128)(2,1)S(1)}, ...), branch_computations={%region_5.5_spmd, %region_6.6_spmd} | conditional | flops 406093824 | bytes 19859568 | solution.py:98
  674.4 66.9 %reduce-scatter.5.cloned.1.call-done = f32[4,128,512]{2,1,0:T(8,128)} async-done(((f32[4,512,512]{2,1,0:T(8,128)}), f32[4,128,512]{2,1,0:T(8,128)}) %reduce-scatter.5.cloned.1.call-update) | async-done | bytes 1048592 | tf_op jit(solution)/shard_map/reduce_scatter | solution.py:129
  743.7 77.2 %reduce-scatter.3.cloned.1.call-done = f32[4,128,512]{2,1,0:T(8,128)} async-done(((f32[4,512,512]{2,1,0:T(8,128)}), f32[4,128,512]{2,1,0:T(8,128)}) %reduce-scatter.3.cloned.1.call-update) | async-done | bytes 1048592 | tf_op jit(solution)/shard_map/reduce_scatter | solution.py:128
  (637 shorter events, 522.1 us)
Async XLA Ops:
  7.2 51.1 %all-gather.3.cloned.1.call-start = ((), (), s32[]{:S(2)}) async-start(), calls=%async_computation.2 | async-start | bytes 2621440 | tf_op jit(solution)/shard_map/all_gather | solution.py:19
  7.9 96.6 %all-gather.5.cloned.1.call-start = ((), (), s32[]{:S(2)}) async-start(), calls=%async_computation.3 | async-start | bytes 2621440 | tf_op jit(solution)/shard_map/all_gather | solution.py:20
  8.6 732.7 %reduce-scatter.5.cloned.1.call-start = ((), (), s32[]{:S(2)}) async-start(), calls=%async_computation.5 | async-start | bytes 5242880 | tf_op jit(solution)/shard_map/reduce_scatter | solution.py:129
  263.4 12.2 %collective-permute-start = (bf16[64,512]{1,0:T(8,128)(2,1)S(1)}, bf16[64,512]{1,0:T(8,128)(2,1)S(1)}, u32[]{:S(2)}, u32[]{:S(2)}) collective-permute-start(bf16[64,512]{1,0:T(8,128)(2,1)S(1)} %get-tuple-element.520), channel_id=1, source_target_pairs={{0,4},{4,8},{8,12},{12,16},{16,20},{20,24},{24,28},{1,5},{5,9},{9,... | collective-permute-start | bytes 196616 | tf_op jit(solution)/shard_map/while/body/eval_jaxpr/ppermute | solution.py:11
  283.9 13.1 %collective-permute-start = (bf16[64,512]{1,0:T(8,128)(2,1)S(1)}, bf16[64,512]{1,0:T(8,128)(2,1)S(1)}, u32[]{:S(2)}, u32[]{:S(2)}) collective-permute-start(bf16[64,512]{1,0:T(8,128)(2,1)S(1)} %get-tuple-element.520), channel_id=1, source_target_pairs={{0,4},{4,8},{8,12},{12,16},{16,20},{20,24},{24,28},{1,5},{5,9},{9,... | collective-permute-start | bytes 196616 | tf_op jit(solution)/shard_map/while/body/eval_jaxpr/ppermute | solution.py:11
  306.2 13.1 %collective-permute-start = (bf16[64,512]{1,0:T(8,128)(2,1)S(1)}, bf16[64,512]{1,0:T(8,128)(2,1)S(1)}, u32[]{:S(2)}, u32[]{:S(2)}) collective-permute-start(bf16[64,512]{1,0:T(8,128)(2,1)S(1)} %get-tuple-element.520), channel_id=1, source_target_pairs={{0,4},{4,8},{8,12},{12,16},{16,20},{20,24},{24,28},{1,5},{5,9},{9,... | collective-permute-start | bytes 196616 | tf_op jit(solution)/shard_map/while/body/eval_jaxpr/ppermute | solution.py:11
  328.5 13.1 %collective-permute-start = (bf16[64,512]{1,0:T(8,128)(2,1)S(1)}, bf16[64,512]{1,0:T(8,128)(2,1)S(1)}, u32[]{:S(2)}, u32[]{:S(2)}) collective-permute-start(bf16[64,512]{1,0:T(8,128)(2,1)S(1)} %get-tuple-element.520), channel_id=1, source_target_pairs={{0,4},{4,8},{8,12},{12,16},{16,20},{20,24},{24,28},{1,5},{5,9},{9,... | collective-permute-start | bytes 196616 | tf_op jit(solution)/shard_map/while/body/eval_jaxpr/ppermute | solution.py:11
  356.5 6.7 collective-permute-start.1
  364.5 6.6 collective-permute-start.1
  372.4 8.5 %collective-permute-start.1 = (bf16[64,512]{1,0:T(8,128)(2,1)S(1)}, bf16[64,512]{1,0:T(8,128)(2,1)S(1)}, u32[]{:S(2)}, u32[]{:S(2)}) collective-permute-start(bf16[64,512]{1,0:T(8,128)(2,1)S(1)} %get-tuple-element.534), channel_id=1, source_target_pairs={{4,0},{8,4},{12,8},{16,12},{20,16},{24,20},{28,24},{5,1},{9,5},{13... | collective-permute-start | bytes 196616 | tf_op jit(solution)/shard_map/while/body/eval_jaxpr/ppermute | solution.py:11
  382.3 6.6 collective-permute-start.1
  390.2 6.6 collective-permute-start.1
  398.1 62.2 %collective-permute-start.1 = (bf16[64,512]{1,0:T(8,128)(2,1)S(1)}, bf16[64,512]{1,0:T(8,128)(2,1)S(1)}, u32[]{:S(2)}, u32[]{:S(2)}) collective-permute-start(bf16[64,512]{1,0:T(8,128)(2,1)S(1)} %get-tuple-element.534), channel_id=1, source_target_pairs={{4,0},{8,4},{12,8},{16,12},{20,16},{24,20},{28,24},{5,1},{9,5},{13... | collective-permute-start | bytes 196616 | tf_op jit(solution)/shard_map/while/body/eval_jaxpr/ppermute | solution.py:11
  470.4 6.6 collective-permute-start.1
  487.1 6.6 collective-permute-start.1
  520.5 6.6 collective-permute-start.1
  537.2 6.6 collective-permute-start.1
  553.9 6.6 collective-permute-start.1
  570.6 6.6 collective-permute-start.1
  587.3 6.6 collective-permute-start.1
  604.0 6.6 collective-permute-start.1
  620.7 6.6 collective-permute-start.1
  637.4 6.6 collective-permute-start.1
  666.7 154.1 %reduce-scatter.3.cloned.1.call-start = ((), (), s32[]{:S(2)}) async-start(), calls=%async_computation.4 | async-start | bytes 5242880 | tf_op jit(solution)/shard_map/reduce_scatter | solution.py:128
  (34 other events, 443.8 us)
Sparse Core Ops, SparseCore 0:
  9.6 48.6 all-gather.2
  59.8 44.6 all-gather.4
  666.9 74.4 reduce-scatter.4
  743.6 77.2 reduce-scatter.2
where the time goes:
time: 839 us; the launch traced here: 830 us
  waiting for transfers between devices  310 us (37%)
  matrix products  171 us (20%)
  starting transfers between devices  121 us (14%)
  local copies, waits for them, and re-layouts  108 us (13%)
  other arithmetic  77.8 us (9%)
  loops' own time  27.8 us (3%)
  between operations  13.8 us (2%)
    ppermute x38, starting transfers between devices, shifted(): lax.ppermute(value, axis, [(source, source + steps) for source in range(i...  121 us
    reduce_scatter x1, waiting for transfers between devices, per_device(): lax.psum_scatter(grad_in, 'dp', scatter_dimension=1, tiled=True)  77.2 us
    dynamic_slice x76, local copies, waits for them, and re-layouts, put(): old = lax.dynamic_index_in_dim(store, index, axis_pos, keepdims=False)  74.4 us
    dot_general x48, matrix products, forward_section(): jnp.dot(hidden, second[layer], preferred_element_type=jnp.float32)  68.7 us
    ppermute x38, waiting for transfers between devices, shifted(): lax.ppermute(value, axis, [(source, source + steps) for source in range(i...  68.3 us
    reduce_scatter x1, waiting for transfers between devices, per_device(): lax.psum_scatter(grad_out, 'dp', scatter_dimension=1, tiled=True)  66.9 us
    dot_general x48, matrix products, backward_section(): pre = jnp.dot(value, first[layer], preferred_element_type=jnp.float32)  50.1 us
    all_gather x1, waiting for transfers between devices, per_device(): lax.all_gather(w_in, 'dp', axis=2, tiled=True)  49.5 us
  transfers between devices with their start and end apart: 42, of which 21 were waited for; matrix products, arithmetic and copies ran while one was open for 16% of the time, Pallas kernels for 0%

commit v1 on v0

--- a/solution.py
+++ b/solution.py
@@ -15,9 +15,37 @@
     sections = lax.axis_size("section")
     place = lax.axis_index("section")
     groups = lax.axis_size("dp")
+
+    def _play_point(block_here, link_axis, along_dim):
+        top, reply, tall = (
+            jax.lax.axis_size(link_axis),
+            jax.lax.axis_index(link_axis),
+            block_here.shape[along_dim],
+        )
+        fields = tuple(((jj, (jj + 1) % top) for jj in range(top)))
+        arrivals = tuple(((jj, (jj - 1) % top) for jj in range(top)))
+        small = jnp.zeros(
+            (*block_here.shape[:along_dim], top * tall, *block_here.shape[along_dim + 1 :]),
+            block_here.dtype,
+        )
+        small = lax.dynamic_update_slice_in_dim(small, block_here, reply * tall, axis=along_dim)
+        out_arr = arr_next = block_here
+        finding = top // 2
+        for k in range(1, finding + 1):
+            out_arr = jax.lax.ppermute(out_arr, axis_name=link_axis, perm=fields)
+            small = lax.dynamic_update_slice_in_dim(
+                small, out_arr, (reply - k) % top * tall, axis=along_dim
+            )
+            if k < top - finding:
+                arr_next = jax.lax.ppermute(arr_next, axis_name=link_axis, perm=arrivals)
+                small = lax.dynamic_update_slice_in_dim(
+                    small, arr_next, (reply + k) % top * tall, axis=along_dim
+                )
+        return small
+
     full_in, full_out = (
         lax.all_gather(w_in, "dp", axis=2, tiled=True),
-        lax.all_gather(w_out, "dp", axis=2, tiled=True),
+        _play_point(w_out, "dp", along_dim=2),
     )
     first = full_in[0]
     second = full_out[0]

time: 839 us -> 797 us (0.950)
  waiting for transfers between devices: 310 us -> 266 us
  matrix products: 171 us -> 159 us
  starting transfers between devices: 121 us -> 132 us
    ppermute x0 -> x3, waiting for transfers between devices: none -> 51.4 us  [the longest x1 33.6 us: _play_point(): arr_next = jax.lax.ppermute(arr_next, axis_name=link_axis, perm=arrivals)]
    all_gather x1 -> x0, waiting for transfers between devices: 46.3 us -> none  [per_device(): lax.all_gather(w_out, 'dp', axis=2, tiled=True)]
    all_gather x1, waiting for transfers between devices: 49.5 us -> 7.71 us  [per_device(): lax.all_gather(w_in, 'dp', axis=2, tiled=True)]
    dot_general x48, matrix products: 26.2 us -> 13.7 us  [backward_section(): lax.dot_general(grad, second[layer], contract, preferred_element_type=jnp...]
    ppermute x0 -> x3, starting transfers between devices: none -> 10.9 us  [the longest x2 8.8 us: _play_point(): out_arr = jax.lax.ppermute(out_arr, axis_name=link_axis, perm=fields)]
  transfers between devices with their start and end apart: 42 -> 44, of which waited for: 21 -> 23; matrix products, arithmetic and copies ran while one was open for 16% -> 17% of each run, Pallas kernels for 0% -> 0%
where the time goes in v1:
time: 797 us; the launch traced here: 788 us
  waiting for transfers between devices  266 us (33%)
  matrix products  159 us (20%)
  starting transfers between devices  132 us (17%)
  local copies, waits for them, and re-layouts  112 us (14%)
  other arithmetic  78 us (10%)
  loops' own time  28 us (4%)
  between operations  13.9 us (2%)
    ppermute x38, starting transfers between devices, shifted(): lax.ppermute(value, axis, [(source, source + steps) for source in range(i...  121 us
    reduce_scatter x1, waiting for transfers between devices, per_device(): lax.psum_scatter(grad_in, 'dp', scatter_dimension=1, tiled=True)  77.3 us
    dynamic_slice x76, local copies, waits for them, and re-layouts, put(): old = lax.dynamic_index_in_dim(store, index, axis_pos, keepdims=False)  74.4 us
    dot_general x48, matrix products, forward_section(): jnp.dot(hidden, second[layer], preferred_element_type=jnp.float32)  68.8 us
    reduce_scatter x1, waiting for transfers between devices, per_device(): lax.psum_scatter(grad_out, 'dp', scatter_dimension=1, tiled=True)  67.5 us
    ppermute x38, waiting for transfers between devices, shifted(): lax.ppermute(value, axis, [(source, source + steps) for source in range(i...  60.9 us
    dot_general x48, matrix products, backward_section(): pre = jnp.dot(value, first[layer], preferred_element_type=jnp.float32)  50.1 us
    dynamic_update_slice x57, other arithmetic, put(): lax.dynamic_update_index_in_dim(store, jnp.where(valid, fresh, old), inde...  47.4 us
  transfers between devices with their start and end apart: 44, of which 23 were waited for; matrix products, arithmetic and copies ran while one was open for 17% of the time, Pallas kernels for 0%

profile of v1, /device:TPU:0, one launch (start us, length us, event | category | flops | bytes accessed | tf_op | source)
XLA Modules:
  0.0 787.9 jit_solution(17002235629283395439)
XLA Ops:
  13.1 14.3 %collective-permute-done.2 = bf16[1,4,128,512]{3,2,1,0:T(8,128)(2,1)S(1)} collective-permute-done((bf16[1,4,128,512]{3,2,1,0:T(8,128)(2,1)}, bf16[1,4,128,512]{3,2,1,0:T(8,128)(2,1)S(1)}, u32[]{:S(2)}, u32[]{:S(2)}) %collective-permute-start.2) | collective-permute-done | bytes 524320 | tf_op jit(solution)/shard_map/ppermute | solution.py:35
  33.5 33.6 %collective-permute-done.3 = bf16[1,4,128,512]{3,2,1,0:T(8,128)(2,1)} collective-permute-done((bf16[1,4,128,512]{3,2,1,0:T(8,128)(2,1)}, bf16[1,4,128,512]{3,2,1,0:T(8,128)(2,1)}, u32[]{:S(2)}, u32[]{:S(2)}) %collective-permute-start.3) | collective-permute-done | bytes 524320 | tf_op jit(solution)/shard_map/ppermute | solution.py:40
  74.1 7.7 all-gather.2.cloned.1.call-done
  84.0 234.7 %while.31 = (s32[]{:T(128)}, bf16[64,512]{1,0:T(8,128)(2,1)S(1)}, bf16[4,12,64,512]{3,2,1,0:T(8,128)(2,1)}, s32[19]{0:T(128)S(1)}, s32[]{:T(128)}, /*index=5*/pr...) while((s32[]{:T(128)}, bf16[64,512]{1,0:T(8,128)(2,1)S(1)}, ...), condition=%wide.region_3.4_spmd, body=%wide.region_0.3_spmd.sunk | while | flops 270106624 | bytes 7408441 | solution.py:110
  240.6 10.5 %collective-permute-start = (bf16[64,512]{1,0:T(8,128)(2,1)S(1)}, bf16[64,512]{1,0:T(8,128)(2,1)S(1)}, u32[]{:S(2)}, u32[]{:S(2)}) collective-permute-start(bf16[64,512]{1,0:T(8,128)(2,1)S(1)} %get-tuple-element.520), channel_id=1, source_target_pairs={{0,4},{4,8},{8,12},{12,16},{16,20},{20,24},{24,28},{1,5},{5,9},{9,... | collective-permute-start | bytes 196616 | tf_op jit(solution)/shard_map/while/body/eval_jaxpr/ppermute | solution.py:11
  261.2 11.3 %collective-permute-start = (bf16[64,512]{1,0:T(8,128)(2,1)S(1)}, bf16[64,512]{1,0:T(8,128)(2,1)S(1)}, u32[]{:S(2)}, u32[]{:S(2)}) collective-permute-start(bf16[64,512]{1,0:T(8,128)(2,1)S(1)} %get-tuple-element.520), channel_id=1, source_target_pairs={{0,4},{4,8},{8,12},{12,16},{16,20},{20,24},{24,28},{1,5},{5,9},{9,... | collective-permute-start | bytes 196616 | tf_op jit(solution)/shard_map/while/body/eval_jaxpr/ppermute | solution.py:11
  283.4 11.4 %collective-permute-start = (bf16[64,512]{1,0:T(8,128)(2,1)S(1)}, bf16[64,512]{1,0:T(8,128)(2,1)S(1)}, u32[]{:S(2)}, u32[]{:S(2)}) collective-permute-start(bf16[64,512]{1,0:T(8,128)(2,1)S(1)} %get-tuple-element.520), channel_id=1, source_target_pairs={{0,4},{4,8},{8,12},{12,16},{16,20},{20,24},{24,28},{1,5},{5,9},{9,... | collective-permute-start | bytes 196616 | tf_op jit(solution)/shard_map/while/body/eval_jaxpr/ppermute | solution.py:11
  305.6 11.3 %collective-permute-start = (bf16[64,512]{1,0:T(8,128)(2,1)S(1)}, bf16[64,512]{1,0:T(8,128)(2,1)S(1)}, u32[]{:S(2)}, u32[]{:S(2)}) collective-permute-start(bf16[64,512]{1,0:T(8,128)(2,1)S(1)} %get-tuple-element.520), channel_id=1, source_target_pairs={{0,4},{4,8},{8,12},{12,16},{16,20},{20,24},{24,28},{1,5},{5,9},{9,... | collective-permute-start | bytes 196616 | tf_op jit(solution)/shard_map/while/body/eval_jaxpr/ppermute | solution.py:11
  324.9 292.5 %while.32 = (s32[]{:T(128)}, bf16[64,512]{1,0:T(8,128)(2,1)S(1)}, bf16[4,12,64,512]{3,2,1,0:T(8,128)(2,1)}, bf16[4,12,64,512]{3,2,1,0:T(8,128)(2,1)}, bf16[4,12,...) while((s32[]{:T(128)}, bf16[64,512]{1,0:T(8,128)(2,1)S(1)}, ...), condition=%wide.region_7.8_spmd, body=%wide.region_4.7_spmd.sunk | while | flops 406487040 | bytes 24055228 | solution.py:142
  381.2 48.9 %collective-permute-done.1 = bf16[64,512]{1,0:T(8,128)(2,1)S(1)} collective-permute-done((bf16[64,512]{1,0:T(8,128)(2,1)S(1)}, bf16[64,512]{1,0:T(8,128)(2,1)S(1)}, u32[]{:S(2)}, u32[]{:S(2)}) %collective-permute-start.1) | collective-permute-done | bytes 65568 | tf_op jit(solution)/shard_map/while/body/eval_jaxpr/ppermute | solution.py:11
  431.4 7.8 conditional.5
  447.0 7.8 conditional.5
  462.7 7.8 conditional.5
  478.3 7.8 conditional.5
  494.0 7.8 conditional.5
  509.7 7.8 conditional.5
  525.4 7.8 conditional.5
  541.0 7.8 conditional.5
  556.7 7.8 conditional.5
  572.3 7.8 conditional.5
  588.0 7.8 conditional.5
  603.7 7.8 conditional.5
  631.7 67.5 %reduce-scatter.5.cloned.1.call-done = f32[4,128,512]{2,1,0:T(8,128)} async-done(((f32[4,512,512]{2,1,0:T(8,128)}), f32[4,128,512]{2,1,0:T(8,128)}) %reduce-scatter.5.cloned.1.call-update) | async-done | bytes 1048592 | tf_op jit(solution)/shard_map/reduce_scatter | solution.py:157
  701.6 77.3 %reduce-scatter.3.cloned.1.call-done = f32[4,128,512]{2,1,0:T(8,128)} async-done(((f32[4,512,512]{2,1,0:T(8,128)}), f32[4,128,512]{2,1,0:T(8,128)}) %reduce-scatter.3.cloned.1.call-update) | async-done | bytes 1048592 | tf_op jit(solution)/shard_map/reduce_scatter | solution.py:156
  (649 shorter events, 533.3 us)
Async XLA Ops:
  7.2 74.6 %all-gather.2.cloned.1.call-start = ((), (), s32[]{:S(2)}) async-start(), calls=%async_computation.2 | async-start | bytes 2621440 | tf_op jit(solution)/shard_map/all_gather | solution.py:47
  7.9 691.3 %reduce-scatter.5.cloned.1.call-start = ((), (), s32[]{:S(2)}) async-start(), calls=%async_computation.4 | async-start | bytes 5242880 | tf_op jit(solution)/shard_map/reduce_scatter | solution.py:157
  8.0 19.5 %collective-permute-start.2 = (bf16[1,4,128,512]{3,2,1,0:T(8,128)(2,1)}, bf16[1,4,128,512]{3,2,1,0:T(8,128)(2,1)S(1)}, u32[]{:S(2)}, u32[]{:S(2)}) collective-permute-start(bf16[1,4,128,512]{3,2,1,0:T(8,128)(2,1)} %param.15), channel_id=1, source_target_pairs={{0,1},{1,2},{2,3},{3,0},{4,5},{5,6},{6,7},{7,4},{8,9},{9,10},{10,1... | collective-permute-start | bytes 1572872 | tf_op jit(solution)/shard_map/ppermute | solution.py:35
  11.0 56.1 %collective-permute-start.3 = (bf16[1,4,128,512]{3,2,1,0:T(8,128)(2,1)}, bf16[1,4,128,512]{3,2,1,0:T(8,128)(2,1)}, u32[]{:S(2)}, u32[]{:S(2)}) collective-permute-start(bf16[1,4,128,512]{3,2,1,0:T(8,128)(2,1)} %param.15), channel_id=1, source_target_pairs={{0,3},{1,0},{2,1},{3,2},{4,7},{5,4},{6,5},{7,6},{8,11},{9,8},{10,9... | collective-permute-start | bytes 1572872 | tf_op jit(solution)/shard_map/ppermute | solution.py:40
  27.4 44.2 %collective-permute-start.4 = (bf16[1,4,128,512]{3,2,1,0:T(8,128)(2,1)S(1)}, bf16[1,4,128,512]{3,2,1,0:T(8,128)(2,1)}, u32[]{:S(2)}, u32[]{:S(2)}) collective-permute-start(bf16[1,4,128,512]{3,2,1,0:T(8,128)(2,1)S(1)} %collective-permute-done.2), channel_id=1, source_target_pairs={{0,1},{1,2},{2,3},{3,0},{4,5},{5,6},{6,7},{7,4},{8,9},{9,10},{10,1... | collective-permute-start | bytes 1572872 | tf_op jit(solution)/shard_map/ppermute | solution.py:35
  240.6 12.2 %collective-permute-start = (bf16[64,512]{1,0:T(8,128)(2,1)S(1)}, bf16[64,512]{1,0:T(8,128)(2,1)S(1)}, u32[]{:S(2)}, u32[]{:S(2)}) collective-permute-start(bf16[64,512]{1,0:T(8,128)(2,1)S(1)} %get-tuple-element.520), channel_id=1, source_target_pairs={{0,4},{4,8},{8,12},{12,16},{16,20},{20,24},{24,28},{1,5},{5,9},{9,... | collective-permute-start | bytes 196616 | tf_op jit(solution)/shard_map/while/body/eval_jaxpr/ppermute | solution.py:11
  261.2 13.1 %collective-permute-start = (bf16[64,512]{1,0:T(8,128)(2,1)S(1)}, bf16[64,512]{1,0:T(8,128)(2,1)S(1)}, u32[]{:S(2)}, u32[]{:S(2)}) collective-permute-start(bf16[64,512]{1,0:T(8,128)(2,1)S(1)} %get-tuple-element.520), channel_id=1, source_target_pairs={{0,4},{4,8},{8,12},{12,16},{16,20},{20,24},{24,28},{1,5},{5,9},{9,... | collective-permute-start | bytes 196616 | tf_op jit(solution)/shard_map/while/body/eval_jaxpr/ppermute | solution.py:11
  283.4 13.1 %collective-permute-start = (bf16[64,512]{1,0:T(8,128)(2,1)S(1)}, bf16[64,512]{1,0:T(8,128)(2,1)S(1)}, u32[]{:S(2)}, u32[]{:S(2)}) collective-permute-start(bf16[64,512]{1,0:T(8,128)(2,1)S(1)} %get-tuple-element.520), channel_id=1, source_target_pairs={{0,4},{4,8},{8,12},{12,16},{16,20},{20,24},{24,28},{1,5},{5,9},{9,... | collective-permute-start | bytes 196616 | tf_op jit(solution)/shard_map/while/body/eval_jaxpr/ppermute | solution.py:11
  305.6 13.1 %collective-permute-start = (bf16[64,512]{1,0:T(8,128)(2,1)S(1)}, bf16[64,512]{1,0:T(8,128)(2,1)S(1)}, u32[]{:S(2)}, u32[]{:S(2)}) collective-permute-start(bf16[64,512]{1,0:T(8,128)(2,1)S(1)} %get-tuple-element.520), channel_id=1, source_target_pairs={{0,4},{4,8},{8,12},{12,16},{16,20},{20,24},{24,28},{1,5},{5,9},{9,... | collective-permute-start | bytes 196616 | tf_op jit(solution)/shard_map/while/body/eval_jaxpr/ppermute | solution.py:11
  333.6 6.6 collective-permute-start.1
  341.6 6.6 collective-permute-start.1
  349.6 8.4 %collective-permute-start.1 = (bf16[64,512]{1,0:T(8,128)(2,1)S(1)}, bf16[64,512]{1,0:T(8,128)(2,1)S(1)}, u32[]{:S(2)}, u32[]{:S(2)}) collective-permute-start(bf16[64,512]{1,0:T(8,128)(2,1)S(1)} %get-tuple-element.534), channel_id=1, source_target_pairs={{4,0},{8,4},{12,8},{16,12},{20,16},{24,20},{28,24},{5,1},{9,5},{13... | collective-permute-start | bytes 196616 | tf_op jit(solution)/shard_map/while/body/eval_jaxpr/ppermute | solution.py:11
  359.4 6.6 collective-permute-start.1
  367.3 6.6 collective-permute-start.1
  375.3 54.8 %collective-permute-start.1 = (bf16[64,512]{1,0:T(8,128)(2,1)S(1)}, bf16[64,512]{1,0:T(8,128)(2,1)S(1)}, u32[]{:S(2)}, u32[]{:S(2)}) collective-permute-start(bf16[64,512]{1,0:T(8,128)(2,1)S(1)} %get-tuple-element.534), channel_id=1, source_target_pairs={{4,0},{8,4},{12,8},{16,12},{20,16},{24,20},{28,24},{5,1},{9,5},{13... | collective-permute-start | bytes 196616 | tf_op jit(solution)/shard_map/while/body/eval_jaxpr/ppermute | solution.py:11
  439.2 6.6 collective-permute-start.1
  454.8 6.6 collective-permute-start.1
  470.5 6.6 collective-permute-start.1
  501.8 6.6 collective-permute-start.1
  517.5 6.6 collective-permute-start.1
  533.2 6.6 collective-permute-start.1
  564.5 6.6 collective-permute-start.1
  595.8 6.6 collective-permute-start.1
  624.1 154.9 %reduce-scatter.3.cloned.1.call-start = ((), (), s32[]{:S(2)}) async-start(), calls=%async_computation.3 | async-start | bytes 5242880 | tf_op jit(solution)/shard_map/reduce_scatter | solution.py:156
  (38 other events, 419.4 us)
Sparse Core Ops, SparseCore 0:
  9.6 72.1 all-gather.1
  624.2 74.9 reduce-scatter.4
  701.7 77.2 reduce-scatter.2
